TPU v7x, 32 devices: a whole 2x2x4 slice. The times are simulated.
32 devices in a mesh: box: 16 (over z, y, x), samp: 2 (over core).
Axes of the slice: x: 2, y: 2, z: 4, core: 2. Of those that a mesh axis runs over, the one named last changes fastest.
Arguments:
- currents: bfloat16 [128, 8, 128], P(('box', 'samp')), may hold values from -6 to 6
- radiation: bfloat16 [128, 2, 2, 512, 128], P(('box', 'samp')), may hold values from -0.1875 to 0.1875
- near_blocks: bfloat16 [128, 8, 2, 128, 128], P(('box', 'samp')), may hold values from -0.125 to 0.125
- near_src: int32 [128, 8], P(('box', 'samp')), may hold values from 0 to 127, as said below
- leaf_parent: int32 [128], P('box'), may hold values from 0 to 255, as said below
- leaf_shift: int32 [128], P('box'), may hold values from 0 to 7
- shift_table: bfloat16 [8, 2, 8192], P(None, None, 'samp'), may hold values from -4 to 4
- interp_idx: int32 [64, 2], P('samp'), may hold values from 0 to 3, as said below
- interp_val: bfloat16 [64, 2, 128, 128], P('samp'), may hold values from -0.375 to 0.375
- top_src: int32 [256, 16], P('box'), may hold values from 0 to 255, as said below
- top_disp: int32 [256, 16], P('box'), may hold values from 0 to 31
- trans_table: bfloat16 [32, 2, 8192], P(None, None, 'samp'), may hold values from -1 to 1
Outputs:
- matvec: float32 [128, 8, 128], P(('box', 'samp'))
Inputs may be any that keep to these rules, and one draw needn't show every extreme that they name: `near_src`: entry 0 of a leaf's row is the leaf itself; every entry lies in the 4 leaves of the leaf's own device or of the devices just before and after it in box+samp order (leaves numbered box-major), and these ends are reached. `leaf_parent`: the parent of leaf l lies in its box group: its value divided by 16 equals l divided by 8. `interp_idx`: the 2 entries of a row differ. `top_src`: a source of top box t is another box of t's group (t // 16), or one of the last 8 boxes of the group before it, or one of the first 8 boxes of the group after it; both rims are reached.
All inputs are finite; a program needn't handle non-finite values.
Results may differ from a plain program's by a relative error of at most 0.013.
Values may be sent and summed in bfloat16 or wider, within the bound.
No kernel may reach another device: no remote copies, remote signals or barrier semaphores. Data moves between devices by JAX's collectives and lax.ppermute only.
A program may use at most 64 MiB of HBM per device.

v0:
```python
import functools

import jax
import jax.numpy as jnp
from jax import lax
from jax.experimental import pallas as pl
from jax.experimental.pallas import tpu as pltpu
from jax.sharding import PartitionSpec as P

F32 = jnp.float32
BF16 = jnp.bfloat16
HBM = pl.BlockSpec(memory_space=pltpu.HBM)
VMEM = pl.BlockSpec(memory_space=pltpu.VMEM)
SMEM = pl.BlockSpec(memory_space=pltpu.SMEM)
NT = (((1,), (1,)), ((), ()))
LIMIT = 14 * 1024 * 1024


def params():
    return pltpu.CompilerParams(vmem_limit_bytes=LIMIT)


def pinned(*arrays):
    return [pltpu.with_memory_space_constraint(array, pltpu.HBM) for array in arrays]


def radiate_kernel(
    parent_hbm,
    shift_hbm,
    cur_hbm,
    rad_hbm,
    phase_hbm,
    trans_hbm,
    msg_ref,
    phase_ref,
    trans_ref,
    parent_ref,
    shift_ref,
    cur_ref,
    rad_ref,
    sem,
    *,
    top_count,
):
    leaf_count, in_blocks = cur_ref.shape[0], msg_ref.shape[0]
    block = msg_ref.shape[2]
    half = cur_ref.shape[1] // 2
    group = parent_ref.shape[0]
    firsts = [
        pltpu.make_async_copy(src, dst, sem.at[leaf_count + n])
        for n, (src, dst) in enumerate(
            ((parent_hbm, parent_ref), (shift_hbm, shift_ref), (cur_hbm, cur_ref))
        )
    ]
    for copy in firsts:
        copy.start()
    copies = [
        pltpu.make_async_copy(rad_hbm.at[leaf], rad_ref.at[leaf], sem.at[leaf])
        for leaf in range(leaf_count)
    ]
    for copy in copies:
        copy.start()
    later = [
        pltpu.make_async_copy(src, dst, sem.at[leaf_count + 3 + n])
        for n, (src, dst) in enumerate(
            ((trans_hbm, trans_ref), (phase_hbm, phase_ref))
        )
    ]
    for copy in later:
        copy.start()
    base = leaf_count * 4 * half
    lane = lax.broadcasted_iota(jnp.int32, (8, block), 1)
    line = lax.broadcasted_iota(jnp.int32, (8, block), 0)
    meta = jnp.zeros((8, block), jnp.int32)
    for copy in firsts:
        copy.wait()
    for member in range(group):
        pair = jnp.where(
            line == 0, lax.rem(parent_ref[member], top_count), shift_ref[member]
        )
        meta = jnp.where(lane == member, pair, meta)
    meta = meta.astype(F32)
    zero = jnp.zeros((half, cur_ref.shape[2]), F32)
    left = []
    for leaf in range(leaf_count):
        cur = cur_ref[leaf].astype(F32)
        real, imag = cur[:half], cur[half:]
        pieces = [
            jnp.concatenate(rows, axis=0).astype(BF16)
            for rows in (
                (real, zero, imag, zero),
                (-imag, zero, real, zero),
                (zero, real, zero, imag),
                (zero, -imag, zero, real),
            )
        ]
        left.append(jnp.concatenate(pieces, axis=1))
        row = base + leaf // in_blocks * 4 * half
        msg_ref[leaf % in_blocks, row : row + 4 * half, :] = jnp.concatenate(
            [cur, meta], axis=0
        ).astype(BF16)
    for leaf in range(leaf_count):
        copies[leaf].wait()
        right = jnp.concatenate(
            [rad_ref[leaf, p, r] for p in range(2) for r in range(2)], axis=1
        )
        out = lax.dot_general(left[leaf], right, NT, preferred_element_type=F32).astype(BF16)
        for b in range(in_blocks):
            msg_ref[b, leaf * 4 * half : (leaf + 1) * 4 * half, :] = out[
                :, b * block : (b + 1) * block
            ]
    for copy in later:
        copy.wait()


def lift_groups(refs, dense_ref, shift_ref, top_ref, rows, base, ready):
    left = jnp.concatenate(
        [
            jnp.concatenate([ref[samp, c, :rows, :] for c in range(ref.shape[1])], axis=1)
            for ref in refs
            for samp in range(ref.shape[0])
        ],
        axis=0,
    )
    local_blocks, _, block = top_ref.shape[2:]
    width = min(4, local_blocks)
    for start in range(0, local_blocks, width):
        moved = lax.dot_general(
            left,
            dense_ref[start * block : (start + width) * block, :],
            NT,
            preferred_element_type=F32,
        )
        if start == 0:
            sids = ready()
        for b in range(width):
            for s, sid in enumerate(sids):
                real = moved[s * 16 : s * 16 + 8, b * block : (b + 1) * block]
                imag = moved[s * 16 + 8 : s * 16 + 16, b * block : (b + 1) * block]
                shift_real, shift_imag = shift_ref[sid, start + b], shift_ref[sid + 1, start + b]
                top_ref[base + s, 0, start + b] = real * shift_real - imag * shift_imag
                top_ref[base + s, 1, start + b] = real * shift_imag + imag * shift_real


def spread_rows(src_ref, out_ref):
    count, local_blocks, block = src_ref.shape

    def one(index, carry):
        for b in range(local_blocks):
            out_ref[index, b] = jnp.broadcast_to(src_ref[index, b : b + 1, :], (8, block))
        return carry

    lax.fori_loop(0, count, one, 0)


def tables_kernel(
    idx_ref,
    sid_ref,
    val_hbm,
    near_hbm,
    here_ref,
    shift_ref,
    trans_ref,
    dense_ref,
    wide_shift_ref,
    wide_trans_ref,
    top_ref,
    near_ref,
    val_ref,
    sem,
    *,
    rows,
):
    load = pltpu.make_async_copy(val_hbm, val_ref, sem.at[0])
    load.start()
    other = pltpu.make_async_copy(near_hbm, near_ref, sem.at[1])
    other.start()
    spread_rows(shift_ref, wide_shift_ref)
    spread_rows(trans_ref, wide_trans_ref)
    last = trans_ref.shape[0]
    wide_trans_ref[last:] = jnp.zeros((2, *wide_trans_ref.shape[1:]), F32)
    load.wait()
    local_blocks, _, block, _ = val_ref.shape

    def one(b, carry):
        first, second = idx_ref[0, b], idx_ref[1, b]
        zero = jnp.zeros((block, block), BF16)
        for c in range(dense_ref.shape[1] // block):
            dense_ref[pl.ds(pl.multiple_of(b * block, block), block), c * block : (c + 1) * block] = (
                jnp.where(first == c, val_ref[b, 0], jnp.where(second == c, val_ref[b, 1], zero))
            )
        return carry

    lax.fori_loop(0, local_blocks, one, 0)
    sids = [2 * sid_ref[s] for s in range(sid_ref.shape[0])]
    lift_groups((here_ref,), dense_ref, wide_shift_ref, top_ref, rows, 0, lambda: sids)
    other.wait()


def meta_of(msg_ref, rows):
    return msg_ref[0, 0, rows : rows + 16, :].astype(F32)[8:10]


def field_kernel(
    parent_hbm,
    sid_hbm,
    src_hbm,
    disp_hbm,
    here_ref,
    near_ref,
    far_ref,
    dense_ref,
    shift_ref,
    trans_ref,
    _,
    *rest,
    n_samp,
    leaf_count,
    tile,
):
    outs = rest[:n_samp]
    (
        top_ref,
        parent_ref,
        sid_ref,
        src_ref,
        disp_ref,
        inc_ref,
        down_ref,
        acc_ref,
        meta_ref,
        num_ref,
        head_ref,
        rep_ref,
        count_ref,
        slot_ref,
        coef_ref,
        sem,
    ) = rest[n_samp:]
    block = here_ref.shape[3]
    local_blocks = top_ref.shape[2]
    leaves = top_ref.shape[0]
    group = leaves // 3
    rows = 16 * leaf_count
    top_count, entries = src_ref.shape
    where = lax.axis_index("box")
    me = lax.axis_index("samp")
    turned = jnp.where(me == 1, 1, 0) if n_samp == 2 else jnp.int32(0)
    bases = (1, 2 * turned, 2 - 2 * turned)

    lines = [meta_of(ref, rows) for ref in (here_ref, near_ref, far_ref)]
    meta_ref[...] = jnp.concatenate(lines + lines[:1], axis=0).astype(jnp.int32)
    fetches = [
        pltpu.make_async_copy(src, dst, sem.at[n])
        for n, (src, dst) in enumerate(
            (
                (parent_hbm, parent_ref),
                (sid_hbm, sid_ref),
                (src_hbm, src_ref),
                (disp_hbm, disp_ref),
                (meta_ref, num_ref),
            )
        )
    ]
    for fetch in fetches:
        fetch.start()
    for box in range(3 * top_count):
        head_ref[box] = -1

    def ready():
        for fetch in fetches:
            fetch.wait()
        return [2 * num_ref[line, s] for line in (3, 5) for s in range(group)]

    lift_groups((near_ref, far_ref), dense_ref, shift_ref, top_ref, rows, group, ready)
    boxes = [
        num_ref[2 * (s // group), s % group] + bases[s // group] * top_count for s in range(leaves)
    ]
    for s in reversed(range(leaves)):
        head_ref[boxes[s]] = s
    for s in range(leaves):
        rep_ref[s] = head_ref[boxes[s]]
    for leaf in range(group):
        parent = parent_ref[leaf] - where * top_count
        count = jnp.int32(0)
        slots = [head_ref[src_ref[parent, j] - (where - 1) * top_count] for j in range(entries)]
        coefs = [2 * disp_ref[parent, j] for j in range(entries)]
        for slot, coef in zip(slots, coefs):
            slot_ref[leaf, count] = slot
            coef_ref[leaf, count] = coef
            count += (slot >= 0).astype(jnp.int32)
        slot_ref[leaf, count] = 0
        coef_ref[leaf, count] = trans_ref.shape[0] - 2
        count_ref[leaf] = lax.div(count + 1, 2)

    def merge(s, carry):
        rep = rep_ref[s]

        @pl.when(rep != s)
        def _():
            top_ref[rep] = top_ref[rep] + top_ref[s]

        return carry

    lax.fori_loop(0, leaves, merge, 0)

    def store_down(leaf, b, real, imag):
        sid = 2 * sid_ref[leaf]
        shift_real, shift_imag = shift_ref[sid, b], shift_ref[sid + 1, b]
        down = jnp.concatenate(
            [
                shift_real * real + shift_imag * imag,
                shift_real * imag - shift_imag * real,
            ],
            axis=0,
        )
        start = pl.multiple_of(leaf * 16, 16)
        down_ref[pl.ds(start, 16), b * block : (b + 1) * block] = down.astype(BF16)

    def target(leaf, carry):
        @pl.when(rep_ref[leaf] == leaf)
        def _():
            for t in range(0, local_blocks, tile):

                def entries_of(n, total):
                    real, imag = list(total[:tile]), list(total[tile:])
                    pair = [
                        (slot_ref[leaf, 2 * n + m], coef_ref[leaf, 2 * n + m]) for m in range(2)
                    ]
                    for b in range(tile):
                        place = t + b
                        for slot, coef in pair:
                            move_real, move_imag = trans_ref[coef, place], trans_ref[coef + 1, place]
                            src_real, src_imag = top_ref[slot, 0, place], top_ref[slot, 1, place]
                            real[b] += move_real * src_real - move_imag * src_imag
                            imag[b] += move_real * src_imag + move_imag * src_real
                    return tuple(real + imag)

                zero = jnp.zeros((8, block), F32)
                total = lax.fori_loop(0, count_ref[leaf], entries_of, (zero,) * (2 * tile))
                for b in range(tile):
                    inc_ref[leaf, 0, t + b] = total[b]
                    inc_ref[leaf, 1, t + b] = total[tile + b]
                    store_down(leaf, t + b, total[b], total[tile + b])

        return carry

    lax.fori_loop(0, group, target, 0)

    def lower(leaf, carry):
        rep = rep_ref[leaf]

        @pl.when(rep != leaf)
        def _():
            for b in range(local_blocks):
                store_down(leaf, b, inc_ref[rep, 0, b], inc_ref[rep, 1, b])

        return carry

    lax.fori_loop(0, group, lower, 0)
    acc_ref[...] = jnp.dot(down_ref[...], dense_ref[...], preferred_element_type=F32)
    for d, out in enumerate(outs):
        owner = lax.rem(me + d, n_samp)
        start = pl.multiple_of(owner * rows, rows)
        for c in range(out.shape[0]):
            out[c] = acc_ref[pl.ds(start, rows), c * block : (c + 1) * block].astype(BF16)


def near_kernel(src_ref, near_ref, here_ref, *rest, rows, n_samp):
    other_refs, out_ref, cur_ref = rest[:-2], rest[-2], rest[-1]
    leaf_count, near = near_ref.shape[:2]
    in_blocks = here_ref.shape[1]
    group = n_samp * leaf_count
    where = lax.axis_index("box")
    turned = jnp.where(lax.axis_index("samp") == 1, 1, 0) if n_samp == 2 else jnp.int32(0)
    places = (1, 2 * turned, 2 - 2 * turned)
    for place, ref in zip(places, (here_ref,) + other_refs):
        for leaf in range(group):
            samp, inner = leaf // leaf_count, leaf % leaf_count
            line = rows + inner // in_blocks * 16
            cur = ref[samp, inner % in_blocks, line : line + 16, :].astype(F32)
            cur_ref[place * group + leaf] = jnp.concatenate(
                [cur[:8], -cur[4:8], cur[:4]], axis=0
            ).astype(BF16)
    for leaf in range(leaf_count):
        left = jnp.concatenate(
            [cur_ref[src_ref[leaf, n] - (where - 1) * group] for n in range(near)], axis=1
        )
        out = [
            lax.dot_general(
                left,
                jnp.concatenate([near_ref[leaf, n, r] for n in range(near)], axis=1),
                NT,
                preferred_element_type=F32,
            )
            for r in range(2)
        ]
        out_ref[leaf] = out[0][:8] + out[1][8:]


def receive_kernel(near_ref, rad_ref, *rest):
    far_refs, out_ref = rest[:-1], rest[-1]
    leaf_count = out_ref.shape[0]
    far = far_refs[0][...].astype(F32)
    for ref in far_refs[1:]:
        far = far + ref[...].astype(F32)
    in_blocks = far.shape[0]
    unknowns = rad_ref.shape[4]
    depth = rad_ref.shape[1] * rad_ref.shape[2] * rad_ref.shape[3]
    for leaf in range(leaf_count):
        left = []
        for p in range(2):
            real = [far[b, leaf * 16 + p * 4 : leaf * 16 + p * 4 + 4] for b in range(in_blocks)]
            imag = [
                far[b, leaf * 16 + 8 + p * 4 : leaf * 16 + 12 + p * 4] for b in range(in_blocks)
            ]
            left += [jnp.concatenate(pair, axis=0) for pair in zip(real, imag)]
            left += [jnp.concatenate([i, -r], axis=0) for r, i in zip(real, imag)]
        wide = jnp.concatenate(left, axis=1).astype(BF16)
        right = rad_ref[leaf].reshape(depth, unknowns)
        out_ref[leaf] = near_ref[leaf] + jnp.dot(wide, right, preferred_element_type=F32)


def per_device(
    currents,
    radiation,
    near_blocks,
    near_src,
    leaf_parent,
    leaf_shift,
    shift_table,
    interp_idx,
    interp_val,
    top_src,
    top_disp,
    trans_table,
):
    n_samp = lax.axis_size("samp")
    n_box = lax.axis_size("box")
    leaf_count, comps, unknowns = currents.shape
    group = leaf_parent.shape[0]
    top_count, entries = top_src.shape
    local_blocks, _, block, _ = interp_val.shape
    in_blocks = radiation.shape[3] // block
    leaves = 3 * group
    rows = 16 * leaf_count
    extra = 16 * -(-leaf_count // in_blocks)
    tile = min(16, local_blocks)

    message, phases, moves = pl.pallas_call(
        functools.partial(radiate_kernel, top_count=top_count),
        out_shape=[
            jax.ShapeDtypeStruct((in_blocks, rows + extra, block), BF16),
            pltpu.VMEM(shift_table.shape, BF16),
            pltpu.VMEM(trans_table.shape, BF16),
        ],
        in_specs=[HBM] * 6,
        out_specs=[VMEM] * 3,
        scratch_shapes=[
            pltpu.SMEM(leaf_parent.shape, jnp.int32),
            pltpu.SMEM(leaf_shift.shape, jnp.int32),
            pltpu.VMEM(currents.shape, BF16),
            pltpu.VMEM(radiation.shape, BF16),
            pltpu.SemaphoreType.DMA((leaf_count + 5,)),
        ],
        compiler_params=params(),
        name="radiate",
    )(
        *pinned(
            leaf_parent, leaf_shift, currents, radiation, shift_table, trans_table
        )
    )

    here = lax.all_gather(message, "samp", axis=0)
    last = n_samp - 1
    swap = []
    for box in range(n_box - 1):
        low, high = box * n_samp + last, (box + 1) * n_samp
        swap += [(low, high), (high, low)]
    beyond = lax.ppermute(here, ("box", "samp"), swap)
    shift_rows = phases.astype(F32).reshape(-1, local_blocks, block)
    trans_rows = moves.astype(F32).reshape(-1, local_blocks, block)
    work = 2 * leaves * 16 * in_blocks * block * local_blocks * block
    top_shape = pltpu.VMEM((leaves, 2, local_blocks, 8, block), F32)
    dense, wide_shift, wide_trans, own_top, near_values = pl.pallas_call(
        functools.partial(tables_kernel, rows=rows),
        out_shape=[
            pltpu.VMEM((local_blocks * block, in_blocks * block), BF16),
            pltpu.VMEM((shift_rows.shape[0], local_blocks, 8, block), F32),
            pltpu.VMEM((trans_rows.shape[0] + 2, local_blocks, 8, block), F32),
            top_shape,
            pltpu.VMEM(near_blocks.shape, BF16),
        ],
        in_specs=[SMEM, SMEM, HBM, HBM] + [VMEM] * 3,
        out_specs=[VMEM] * 5,
        scratch_shapes=[pltpu.VMEM(interp_val.shape, BF16), pltpu.SemaphoreType.DMA((2,))],
        compiler_params=params(),
        cost_estimate=pl.CostEstimate(flops=work, bytes_accessed=1 << 24, transcendentals=0),
        name="tables",
    )(interp_idx.T, leaf_shift, *pinned(interp_val, near_blocks), here, shift_rows, trans_rows)
    beyond, dense = lax.optimization_barrier((beyond, dense))
    if n_samp == 2:
        first = beyond
        second = lax.ppermute(beyond, "samp", [(0, 1), (1, 0)])
    else:
        ends = lax.all_gather(beyond, "samp", axis=0)
        first, second = ends[0], ends[n_samp - 1]
    numbers = [pltpu.VMEM((8, block), jnp.int32), pltpu.SMEM((8, block), jnp.int32)]
    sources = (here, first) if n_samp == 2 else (here, first, second)
    near_out = pl.pallas_call(
        functools.partial(near_kernel, rows=rows, n_samp=n_samp),
        out_shape=jax.ShapeDtypeStruct((leaf_count, comps, unknowns), F32),
        in_specs=[SMEM] + [VMEM] * (1 + len(sources)),
        out_specs=VMEM,
        scratch_shapes=[pltpu.VMEM((leaves, 16, block), BF16)],
        compiler_params=params(),
        cost_estimate=pl.CostEstimate(flops=work, bytes_accessed=1 << 22, transcendentals=0),
        name="near",
    )(near_src, near_values, *sources)
    second, near_out = lax.optimization_barrier((second, near_out))

    *fars, _ = pl.pallas_call(
        functools.partial(field_kernel, n_samp=n_samp, leaf_count=leaf_count, tile=tile),
        out_shape=[jax.ShapeDtypeStruct((in_blocks, rows, block), BF16)] * n_samp
        + [top_shape],
        in_specs=[HBM] * 4 + [VMEM] * 7,
        out_specs=[VMEM] * (n_samp + 1),
        scratch_shapes=[
            pltpu.SMEM(leaf_parent.shape, jnp.int32),
            pltpu.SMEM(leaf_shift.shape, jnp.int32),
            pltpu.SMEM(top_src.shape, jnp.int32),
            pltpu.SMEM(top_disp.shape, jnp.int32),
            pltpu.VMEM((group, 2, local_blocks, 8, block), F32),
            pltpu.VMEM((group * 16, local_blocks * block), BF16),
            pltpu.VMEM((group * 16, in_blocks * block), F32),
            *numbers,
            pltpu.SMEM((3 * top_count,), jnp.int32),
            pltpu.SMEM((leaves,), jnp.int32),
            pltpu.SMEM((group,), jnp.int32),
            pltpu.SMEM((group, entries + 1), jnp.int32),
            pltpu.SMEM((group, entries + 1), jnp.int32),
            pltpu.SemaphoreType.DMA((5,)),
        ],
        input_output_aliases={10: n_samp},
        compiler_params=params(),
        name="field",
    )(
        *pinned(leaf_parent, leaf_shift, top_src, top_disp),
        here,
        first,
        second,
        dense,
        wide_shift,
        wide_trans,
        own_top,
    )
    received = [fars[0]] + [
        lax.ppermute(fars[d], "samp", [(i, (i + d) % n_samp) for i in range(n_samp)])
        for d in range(1, n_samp)
    ]
    return pl.pallas_call(
        receive_kernel,
        out_shape=jax.ShapeDtypeStruct((leaf_count, comps, unknowns), F32),
        in_specs=[VMEM] * (2 + n_samp),
        out_specs=VMEM,
        compiler_params=params(),
        name="receive",
    )(near_out, radiation, *received)


def solution(mesh):
    placed = (
        P(("box", "samp"), None, None),
        P(("box", "samp"), None, None, None, None),
        P(("box", "samp"), None, None, None, None),
        P(("box", "samp"), None),
        P("box"),
        P("box"),
        P(None, None, "samp"),
        P("samp", None),
        P("samp", None, None, None),
        P("box", None),
        P("box", None),
        P(None, None, "samp"),
    )
    return jax.shard_map(
        per_device,
        mesh=mesh,
        in_specs=placed,
        out_specs=P(("box", "samp"), None, None),
        check_vma=False,
    )
```

profile of v0, /device:TPU:0, one launch (start us, length us, event | category | flops | bytes accessed | tf_op | source)
XLA Modules:
  0.0 26.5 jit_solution(15265880294761278281)
XLA Ops:
  0.0 0.0 copy-start.1
  0.0 0.0 copy-start.3
  0.0 2.2 %radiate.1 = (bf16[4,80,128]{2,1,0:T(8,128)(2,1)S(1)}, bf16[8,2,4096]{2,1,0:T(2,128)(2,1)S(1)}, bf16[32,2,4096]{2,1,0:T(2,128)(2,1)S(1)}) custom-call(s32[8]{0:T(128)} %parent_hbm.3, s32[8]{0:T(128)} %sid_hbm.1, bf16[4,8,128]{2,1,0:T(8,128)(2,1)} %cur_hbm.1, bf16[4,2,2,512,128]{4,3,2,1,0:T(8,128)(2,1)} %rad_ref.1, bf16[8,2,4096]{2,1,0:T(2,128)(2,1)} %phase_hbm.1, ...), custom_call_target="tpu_custom_call" | custom-call | tf_op jit(solution)/shard_map/radiate/pallas_call | solution.py:450
  2.2 2.0 %all-gather = bf16[8,80,128]{2,1,0:T(8,128)(2,1)S(1)} all-gather(bf16[4,80,128]{2,1,0:T(8,128)(2,1)S(1)} %get-tuple-element.19), channel_id=2, replica_groups=mesh['box'=16,'samp'=2] {'samp'}, dimensions={0}, use_global_device_ids=true | all-gather | bytes 245760 | tf_op jit(solution)/shard_map/all_gather | solution.py:474
  4.2 0.7 %collective-permute-start = (bf16[2,4,80,128]{3,2,1,0:T(8,128)(2,1)S(1)}, bf16[2,4,80,128]{3,2,1,0:T(8,128)(2,1)S(1)}, u32[]{:S(2)}, u32[]{:S(2)}) collective-permute-start(bf16[2,4,80,128]{3,2,1,0:T(8,128)(2,1)S(1)} %bitcast.2), channel_id=1, source_target_pairs={{1,2},{2,1},{3,4},{4,3},{5,6},{6,5},{7,8},{8,7},{9,10},{10,9},{11,... | collective-permute-start | bytes 491528 | tf_op jit(solution)/shard_map/ppermute | solution.py:480
  4.9 0.1 reshape.15.shift_ref
  5.0 0.3 %reshape.17.trans_ref = f32[64,32,128]{2,1,0:T(8,128)S(1)} reshape(bf16[32,2,4096]{2,1,0:T(2,128)(2,1)S(1)} %get-tuple-element.21) | data formatting | bytes 1572864 | tf_op jit(solution)/shard_map/reshape | solution.py:482
  5.3 0.0 copy-done.1
  5.3 0.0 copy-done.3
  5.3 0.0 copy-start.2
  5.4 4.7 %tables.1 = (bf16[4096,512]{1,0:T(8,128)(2,1)S(1)}, f32[16,32,8,128]{3,2,1,0:T(8,128)S(1)}, f32[66,32,8,128]{3,2,1,0:T(8,128)S(1)}, f32[24,2,32,8,128]{4,3,2,1,0:T(8,128)S(1)}, bf16[4,8,2,128,128]{4,3,2,1,0:T(8,128)(2,1)S(1)}) custom-call(s32[2,32]{1,0:T(2,128)S(1)} %bitcast.6, s32[8]{0:T(128)S(1)} %copy-done.1, bf16[32,2,128,128]{3,2,1,0:T(8,128)(2,1)} %val_hbm.1, ...), custom_call_target="tpu_custom_call" | custom-call | flops 1610612736 | bytes 16777216 | tf_op jit(solution)/shard_map/tables/pallas_call | solution.py:485
  10.0 0.0 collective-permute-done.rest_0_.near_ref
  10.0 4.3 %collective-permute-start.1 = (bf16[2,4,80,128]{3,2,1,0:T(8,128)(2,1)S(1)}, bf16[2,4,80,128]{3,2,1,0:T(8,128)(2,1)S(1)}, u32[]{:S(2)}, u32[]{:S(2)}) collective-permute-start(bf16[2,4,80,128]{3,2,1,0:T(8,128)(2,1)S(1)} %collective-permute-done.rest_0_.near_ref), channel_id=1, source_target_pairs={{0,1},{1,0},{2,3},{3,2},{4,5},{5,4},{6,7},{7,6},{8,9},{9,8},{10,11... | collective-permute-start | bytes 491528 | tf_op jit(solution)/shard_map/ppermute | solution.py:504
  14.3 0.0 copy-done.2
  14.3 1.2 %near.1.near_ref = f32[4,8,128]{2,1,0:T(8,128)S(1)} custom-call(s32[4,8]{1,0:T(4,128)S(1)} %copy-done.2, bf16[4,8,2,128,128]{4,3,2,1,0:T(8,128)(2,1)S(1)} %get-tuple-element.24.near_ref, bf16[2,4,80,128]{3,2,1,0:T(8,128)(2,1)S(1)} %bitcast.4, bf16[2,4,80,128]{3,2,1,0:T(8,128)(2,1)S(1)} %collective-permute-done.rest_0_.near_ref), custom_call_target="tpu_custom_call" | custom-call | flops 1610612736 | bytes 4194304 | tf_op jit(solution)/shard_map/near/pallas_call | solution.py:510
  15.5 0.0 collective-permute-done.1.far_ref
  15.5 0.0 copy-start
  15.5 8.7 %field.1 = (bf16[4,64,128]{2,1,0:T(8,128)(2,1)S(1)}, bf16[4,64,128]{2,1,0:T(8,128)(2,1)S(1)}, f32[24,2,32,8,128]{4,3,2,1,0:T(8,128)S(1)}) custom-call(s32[8]{0:T(128)} %parent_hbm.3, s32[8]{0:T(128)} %sid_hbm.1, s32[16,16]{1,0:T(8,128)} %src_hbm.1, s32[16,16]{1,0:T(8,128)} %disp_hbm.1, ...), custom_call_target="tpu_custom_call", output_to_operand_aliasing={{2}: (10, {})} | custom-call | tf_op jit(solution)/shard_map/field/pallas_call | solution.py:522
  24.2 0.2 collective-permute-start.2
  24.4 1.1 %collective-permute-done.2.rest_1_ = bf16[4,64,128]{2,1,0:T(8,128)(2,1)S(1)} collective-permute-done((bf16[4,64,128]{2,1,0:T(8,128)(2,1)S(1)}, bf16[4,64,128]{2,1,0:T(8,128)(2,1)S(1)}, u32[]{:S(2)}, u32[]{:S(2)}) %collective-permute-start.2) | collective-permute-done | bytes 65568 | tf_op jit(solution)/shard_map/ppermute | solution.py:558
  25.5 0.0 copy-done
  25.5 1.0 %receive.1 = f32[4,8,128]{2,1,0:T(8,128)} custom-call(f32[4,8,128]{2,1,0:T(8,128)S(1)} %near.1.near_ref, bf16[4,2,2,512,128]{4,3,2,1,0:T(8,128)(2,1)S(1)} %copy-done, bf16[4,64,128]{2,1,0:T(8,128)(2,1)S(1)} %get-tuple-element.31.rest_0_, bf16[4,64,128]{2,1,0:T(8,128)(2,1)S(1)} %collective-permute-done.2.rest_1_), custom_call_target="tpu_custom_call" | custom-call | tf_op jit(solution)/shard_map/receive/pallas_call | solution.py:561
Async XLA Ops:
  0.0 5.3 %copy-start.1 = (s32[8]{0:T(128)S(1)}, s32[8]{0:T(128)}, u32[]{:S(2)}) copy-start(s32[8]{0:T(128)} %sid_hbm.1) | copy-start | bytes 100
  0.0 5.3 %copy-start.3 = (s32[32,2]{0,1:T(2,128)S(1)}, s32[32,2]{0,1:T(2,128)}, u32[]{:S(2)}) copy-start(s32[32,2]{0,1:T(2,128)} %param.19) | copy-start | bytes 772
  4.2 5.8 %collective-permute-start = (bf16[2,4,80,128]{3,2,1,0:T(8,128)(2,1)S(1)}, bf16[2,4,80,128]{3,2,1,0:T(8,128)(2,1)S(1)}, u32[]{:S(2)}, u32[]{:S(2)}) collective-permute-start(bf16[2,4,80,128]{3,2,1,0:T(8,128)(2,1)S(1)} %bitcast.2), channel_id=1, source_target_pairs={{1,2},{2,1},{3,4},{4,3},{5,6},{6,5},{7,8},{8,7},{9,10},{10,9},{11,... | collective-permute-start | bytes 491528 | tf_op jit(solution)/shard_map/ppermute | solution.py:480
  5.3 8.9 %copy-start.2 = (s32[4,8]{1,0:T(4,128)S(1)}, s32[4,8]{1,0:T(4,128)}, u32[]{:S(2)}) copy-start(s32[4,8]{1,0:T(4,128)} %src_ref.1) | copy-start | bytes 388
  10.0 5.5 %collective-permute-start.1 = (bf16[2,4,80,128]{3,2,1,0:T(8,128)(2,1)S(1)}, bf16[2,4,80,128]{3,2,1,0:T(8,128)(2,1)S(1)}, u32[]{:S(2)}, u32[]{:S(2)}) collective-permute-start(bf16[2,4,80,128]{3,2,1,0:T(8,128)(2,1)S(1)} %collective-permute-done.rest_0_.near_ref), channel_id=1, source_target_pairs={{0,1},{1,0},{2,3},{3,2},{4,5},{5,4},{6,7},{7,6},{8,9},{9,8},{10,11... | collective-permute-start | bytes 491528 | tf_op jit(solution)/shard_map/ppermute | solution.py:504
  15.5 10.0 %copy-start = (bf16[4,2,2,512,128]{4,3,2,1,0:T(8,128)(2,1)S(1)}, bf16[4,2,2,512,128]{4,3,2,1,0:T(8,128)(2,1)}, u32[]{:S(2)}) copy-start(bf16[4,2,2,512,128]{4,3,2,1,0:T(8,128)(2,1)} %rad_ref.1) | copy-start | bytes 6291460
  24.2 1.3 %collective-permute-start.2 = (bf16[4,64,128]{2,1,0:T(8,128)(2,1)S(1)}, bf16[4,64,128]{2,1,0:T(8,128)(2,1)S(1)}, u32[]{:S(2)}, u32[]{:S(2)}) collective-permute-start(bf16[4,64,128]{2,1,0:T(8,128)(2,1)S(1)} %get-tuple-element.32), channel_id=1, source_target_pairs={{0,1},{1,0},{2,3},{3,2},{4,5},{5,4},{6,7},{7,6},{8,9},{9,8},{10,11... | collective-permute-start | bytes 196616 | tf_op jit(solution)/shard_map/ppermute | solution.py:558
where the time goes:
time: 26.4 us; the launch traced here: 26.5 us
  Pallas kernels  17.7 us (67%)
  starting transfers between devices  5.15 us (20%)
  blocking collectives  2.02 us (8%)
  waiting for transfers between devices  1.09 us (4%)
  local copies, waits for them, and re-layouts  0.45 us (2%)
    pallas_call x1, Pallas kernels, per_device(): pl.pallas_call(functools.partial(field_kernel, n_samp=n_samp, leaf_count=...  8.68 us
    pallas_call x1, Pallas kernels, per_device(): pl.pallas_call(functools.partial(tables_kernel, rows=rows), out_shape=[pl...  4.65 us
    ppermute x1, starting transfers between devices, per_device(): second = lax.ppermute(beyond, 'samp', [(0, 1), (1, 0)])  4.26 us
    pallas_call x1, Pallas kernels, per_device(): pl.pallas_call(functools.partial(radiate_kernel, top_count=top_count), ou...  2.18 us
    all_gather x1, blocking collectives, per_device(): here = lax.all_gather(message, 'samp', axis=0)  2.02 us
    pallas_call x1, Pallas kernels, per_device(): pl.pallas_call(functools.partial(near_kernel, rows=rows, n_samp=n_samp),...  1.2 us
    ppermute x1, waiting for transfers between devices, per_device(): lax.ppermute(fars[d], 'samp', [(i, (i + d) % n_samp) for i in range(n_sam...  1.09 us
    pallas_call x1, Pallas kernels, per_device(): pl.pallas_call(receive_kernel, out_shape=jax.ShapeDtypeStruct((leaf_count...  1 us
  transfers between devices with their start and end apart: 3, of which 1 were waited for; matrix products, arithmetic and copies ran while one was open for 2% of the time, Pallas kernels for 22%

commit v1 on v0

--- a/solution.py
+++ b/solution.py
@@ -123,7 +123,7 @@
         axis=0,
     )
     local_blocks, _, block = top_ref.shape[2:]
-    width = min(4, local_blocks)
+    width = min(2, local_blocks)
     for start in range(0, local_blocks, width):
         moved = lax.dot_general(
             left,

time: 26.4 us -> 25.8 us (0.977)
  the two profiles are of different devices: /device:TPU:0 before, /device:TPU:25 now
where the time goes in v1:
time: 25.8 us
  Pallas kernels  17.3 us (67%)
  starting transfers between devices  4.63 us (18%)
  blocking collectives  2.24 us (9%)
  waiting for transfers between devices  1.1 us (4%)
  local copies, waits for them, and re-layouts  0.45 us (2%)
    pallas_call x1, Pallas kernels, per_device(): pl.pallas_call(functools.partial(field_kernel, n_samp=n_samp, leaf_count=...  8.21 us
    pallas_call x1, Pallas kernels, per_device(): pl.pallas_call(functools.partial(tables_kernel, rows=rows), out_shape=[pl...  4.65 us
    ppermute x1, starting transfers between devices, per_device(): beyond = lax.ppermute(here, ('box', 'samp'), swap)  3.35 us
    all_gather x1, blocking collectives, per_device(): here = lax.all_gather(message, 'samp', axis=0)  2.24 us
    pallas_call x1, Pallas kernels, per_device(): pl.pallas_call(functools.partial(radiate_kernel, top_count=top_count), ou...  2.18 us
    pallas_call x1, Pallas kernels, per_device(): pl.pallas_call(functools.partial(near_kernel, rows=rows, n_samp=n_samp),...  1.2 us
    ppermute x1, waiting for transfers between devices, per_device(): lax.ppermute(fars[d], 'samp', [(i, (i + d) % n_samp) for i in range(n_sam...  1.1 us
    ppermute x1, starting transfers between devices, per_device(): second = lax.ppermute(beyond, 'samp', [(0, 1), (1, 0)])  1.06 us
  transfers between devices with their start and end apart: 3, of which 1 were waited for; matrix products, arithmetic and copies ran while one was open for 2% of the time, Pallas kernels for 23%

profile of v1, /device:TPU:25, one launch (start us, length us, event | category | flops | bytes accessed | tf_op | source)
XLA Modules:
  0.0 25.8 jit_solution(3772040892196437037)
XLA Ops:
  0.0 0.0 copy-start.1
  0.0 0.0 copy-start.3
  0.0 2.2 %radiate.1 = (bf16[4,80,128]{2,1,0:T(8,128)(2,1)S(1)}, bf16[8,2,4096]{2,1,0:T(2,128)(2,1)S(1)}, bf16[32,2,4096]{2,1,0:T(2,128)(2,1)S(1)}) custom-call(s32[8]{0:T(128)} %parent_hbm.3, s32[8]{0:T(128)} %sid_hbm.1, bf16[4,8,128]{2,1,0:T(8,128)(2,1)} %cur_hbm.1, bf16[4,2,2,512,128]{4,3,2,1,0:T(8,128)(2,1)} %rad_ref.1, bf16[8,2,4096]{2,1,0:T(2,128)(2,1)} %phase_hbm.1, ...), custom_call_target="tpu_custom_call" | custom-call | tf_op jit(solution)/shard_map/radiate/pallas_call | solution.py:450
  2.2 2.2 %all-gather = bf16[8,80,128]{2,1,0:T(8,128)(2,1)S(1)} all-gather(bf16[4,80,128]{2,1,0:T(8,128)(2,1)S(1)} %get-tuple-element.19), channel_id=2, replica_groups=mesh['box'=16,'samp'=2] {'samp'}, dimensions={0}, use_global_device_ids=true | all-gather | bytes 245760 | tf_op jit(solution)/shard_map/all_gather | solution.py:474
  4.4 3.3 %collective-permute-start = (bf16[2,4,80,128]{3,2,1,0:T(8,128)(2,1)S(1)}, bf16[2,4,80,128]{3,2,1,0:T(8,128)(2,1)S(1)}, u32[]{:S(2)}, u32[]{:S(2)}) collective-permute-start(bf16[2,4,80,128]{3,2,1,0:T(8,128)(2,1)S(1)} %bitcast.2), channel_id=1, source_target_pairs={{1,2},{2,1},{3,4},{4,3},{5,6},{6,5},{7,8},{8,7},{9,10},{10,9},{11,... | collective-permute-start | bytes 491528 | tf_op jit(solution)/shard_map/ppermute | solution.py:480
  7.8 0.1 reshape.15.shift_ref
  7.9 0.3 %reshape.17.trans_ref = f32[64,32,128]{2,1,0:T(8,128)S(1)} reshape(bf16[32,2,4096]{2,1,0:T(2,128)(2,1)S(1)} %get-tuple-element.21) | data formatting | bytes 1572864 | tf_op jit(solution)/shard_map/reshape | solution.py:482
  8.2 0.0 copy-done.1
  8.2 0.0 copy-done.3
  8.3 0.0 copy-start.2
  8.3 4.7 %tables.1 = (bf16[4096,512]{1,0:T(8,128)(2,1)S(1)}, f32[16,32,8,128]{3,2,1,0:T(8,128)S(1)}, f32[66,32,8,128]{3,2,1,0:T(8,128)S(1)}, f32[24,2,32,8,128]{4,3,2,1,0:T(8,128)S(1)}, bf16[4,8,2,128,128]{4,3,2,1,0:T(8,128)(2,1)S(1)}) custom-call(s32[2,32]{1,0:T(2,128)S(1)} %bitcast.6, s32[8]{0:T(128)S(1)} %copy-done.1, bf16[32,2,128,128]{3,2,1,0:T(8,128)(2,1)} %val_hbm.1, ...), custom_call_target="tpu_custom_call" | custom-call | flops 1610612736 | bytes 16777216 | tf_op jit(solution)/shard_map/tables/pallas_call | solution.py:485
  12.9 0.0 collective-permute-done.rest_0_.near_ref
  12.9 1.1 %collective-permute-start.1 = (bf16[2,4,80,128]{3,2,1,0:T(8,128)(2,1)S(1)}, bf16[2,4,80,128]{3,2,1,0:T(8,128)(2,1)S(1)}, u32[]{:S(2)}, u32[]{:S(2)}) collective-permute-start(bf16[2,4,80,128]{3,2,1,0:T(8,128)(2,1)S(1)} %collective-permute-done.rest_0_.near_ref), channel_id=1, source_target_pairs={{0,1},{1,0},{2,3},{3,2},{4,5},{5,4},{6,7},{7,6},{8,9},{9,8},{10,11... | collective-permute-start | bytes 491528 | tf_op jit(solution)/shard_map/ppermute | solution.py:504
  14.0 0.0 copy-done.2
  14.0 1.2 %near.1.near_ref = f32[4,8,128]{2,1,0:T(8,128)S(1)} custom-call(s32[4,8]{1,0:T(4,128)S(1)} %copy-done.2, bf16[4,8,2,128,128]{4,3,2,1,0:T(8,128)(2,1)S(1)} %get-tuple-element.24.near_ref, bf16[2,4,80,128]{3,2,1,0:T(8,128)(2,1)S(1)} %bitcast.4, bf16[2,4,80,128]{3,2,1,0:T(8,128)(2,1)S(1)} %collective-permute-done.rest_0_.near_ref), custom_call_target="tpu_custom_call" | custom-call | flops 1610612736 | bytes 4194304 | tf_op jit(solution)/shard_map/near/pallas_call | solution.py:510
  15.2 0.0 collective-permute-done.1.far_ref
  15.2 0.0 copy-start
  15.2 8.2 %field.1 = (bf16[4,64,128]{2,1,0:T(8,128)(2,1)S(1)}, bf16[4,64,128]{2,1,0:T(8,128)(2,1)S(1)}, f32[24,2,32,8,128]{4,3,2,1,0:T(8,128)S(1)}) custom-call(s32[8]{0:T(128)} %parent_hbm.3, s32[8]{0:T(128)} %sid_hbm.1, s32[16,16]{1,0:T(8,128)} %src_hbm.1, s32[16,16]{1,0:T(8,128)} %disp_hbm.1, ...), custom_call_target="tpu_custom_call", output_to_operand_aliasing={{2}: (10, {})} | custom-call | tf_op jit(solution)/shard_map/field/pallas_call | solution.py:522
  23.4 0.2 collective-permute-start.2
  23.7 1.1 %collective-permute-done.2.rest_1_ = bf16[4,64,128]{2,1,0:T(8,128)(2,1)S(1)} collective-permute-done((bf16[4,64,128]{2,1,0:T(8,128)(2,1)S(1)}, bf16[4,64,128]{2,1,0:T(8,128)(2,1)S(1)}, u32[]{:S(2)}, u32[]{:S(2)}) %collective-permute-start.2) | collective-permute-done | bytes 65568 | tf_op jit(solution)/shard_map/ppermute | solution.py:558
  24.8 0.0 copy-done
  24.8 1.0 %receive.1 = f32[4,8,128]{2,1,0:T(8,128)} custom-call(f32[4,8,128]{2,1,0:T(8,128)S(1)} %near.1.near_ref, bf16[4,2,2,512,128]{4,3,2,1,0:T(8,128)(2,1)S(1)} %copy-done, bf16[4,64,128]{2,1,0:T(8,128)(2,1)S(1)} %get-tuple-element.31.rest_0_, bf16[4,64,128]{2,1,0:T(8,128)(2,1)S(1)} %collective-permute-done.2.rest_1_), custom_call_target="tpu_custom_call" | custom-call | tf_op jit(solution)/shard_map/receive/pallas_call | solution.py:561
Async XLA Ops:
  0.0 8.2 %copy-start.1 = (s32[8]{0:T(128)S(1)}, s32[8]{0:T(128)}, u32[]{:S(2)}) copy-start(s32[8]{0:T(128)} %sid_hbm.1) | copy-start | bytes 100
  0.0 8.2 %copy-start.3 = (s32[32,2]{0,1:T(2,128)S(1)}, s32[32,2]{0,1:T(2,128)}, u32[]{:S(2)}) copy-start(s32[32,2]{0,1:T(2,128)} %param.19) | copy-start | bytes 772
  4.4 8.5 %collective-permute-start = (bf16[2,4,80,128]{3,2,1,0:T(8,128)(2,1)S(1)}, bf16[2,4,80,128]{3,2,1,0:T(8,128)(2,1)S(1)}, u32[]{:S(2)}, u32[]{:S(2)}) collective-permute-start(bf16[2,4,80,128]{3,2,1,0:T(8,128)(2,1)S(1)} %bitcast.2), channel_id=1, source_target_pairs={{1,2},{2,1},{3,4},{4,3},{5,6},{6,5},{7,8},{8,7},{9,10},{10,9},{11,... | collective-permute-start | bytes 491528 | tf_op jit(solution)/shard_map/ppermute | solution.py:480
  8.3 5.7 %copy-start.2 = (s32[4,8]{1,0:T(4,128)S(1)}, s32[4,8]{1,0:T(4,128)}, u32[]{:S(2)}) copy-start(s32[4,8]{1,0:T(4,128)} %src_ref.1) | copy-start | bytes 388
  12.9 2.3 %collective-permute-start.1 = (bf16[2,4,80,128]{3,2,1,0:T(8,128)(2,1)S(1)}, bf16[2,4,80,128]{3,2,1,0:T(8,128)(2,1)S(1)}, u32[]{:S(2)}, u32[]{:S(2)}) collective-permute-start(bf16[2,4,80,128]{3,2,1,0:T(8,128)(2,1)S(1)} %collective-permute-done.rest_0_.near_ref), channel_id=1, source_target_pairs={{0,1},{1,0},{2,3},{3,2},{4,5},{5,4},{6,7},{7,6},{8,9},{9,8},{10,11... | collective-permute-start | bytes 491528 | tf_op jit(solution)/shard_map/ppermute | solution.py:504
  15.2 9.5 %copy-start = (bf16[4,2,2,512,128]{4,3,2,1,0:T(8,128)(2,1)S(1)}, bf16[4,2,2,512,128]{4,3,2,1,0:T(8,128)(2,1)}, u32[]{:S(2)}) copy-start(bf16[4,2,2,512,128]{4,3,2,1,0:T(8,128)(2,1)} %rad_ref.1) | copy-start | bytes 6291460
  23.4 1.3 %collective-permute-start.2 = (bf16[4,64,128]{2,1,0:T(8,128)(2,1)S(1)}, bf16[4,64,128]{2,1,0:T(8,128)(2,1)S(1)}, u32[]{:S(2)}, u32[]{:S(2)}) collective-permute-start(bf16[4,64,128]{2,1,0:T(8,128)(2,1)S(1)} %get-tuple-element.32), channel_id=1, source_target_pairs={{0,1},{1,0},{2,3},{3,2},{4,5},{5,4},{6,7},{7,6},{8,9},{9,8},{10,11... | collective-permute-start | bytes 196616 | tf_op jit(solution)/shard_map/ppermute | solution.py:558

commit v2 on v0

--- a/solution.py
+++ b/solution.py
@@ -293,16 +293,15 @@
         coef_ref[leaf, count] = trans_ref.shape[0] - 2
         count_ref[leaf] = lax.div(count + 1, 2)
 
-    def merge(s, carry):
+    def merge(s):
         rep = rep_ref[s]
 
         @pl.when(rep != s)
         def _():
             top_ref[rep] = top_ref[rep] + top_ref[s]
 
-        return carry
-
-    lax.fori_loop(0, leaves, merge, 0)
+    for s in range(1, leaves):
+        merge(s)
 
     def store_down(leaf, b, real, imag):
         sid = 2 * sid_ref[leaf]

time: 26.4 us -> 26.1 us (0.989)
  no operation moved by 1% of the time
where the time goes in v2:
time: 26.1 us; the launch traced here: 26.5 us
  Pallas kernels  17.7 us (68%)
  starting transfers between devices  5.14 us (20%)
  blocking collectives  2.02 us (8%)
  waiting for transfers between devices  1.1 us (4%)
  local copies, waits for them, and re-layouts  0.45 us (2%)
    pallas_call x1, Pallas kernels, per_device(): pl.pallas_call(functools.partial(field_kernel, n_samp=n_samp, leaf_count=...  8.62 us
    pallas_call x1, Pallas kernels, per_device(): pl.pallas_call(functools.partial(tables_kernel, rows=rows), out_shape=[pl...  4.65 us
    ppermute x1, starting transfers between devices, per_device(): second = lax.ppermute(beyond, 'samp', [(0, 1), (1, 0)])  4.26 us
    pallas_call x1, Pallas kernels, per_device(): pl.pallas_call(functools.partial(radiate_kernel, top_count=top_count), ou...  2.18 us
    all_gather x1, blocking collectives, per_device(): here = lax.all_gather(message, 'samp', axis=0)  2.02 us
    pallas_call x1, Pallas kernels, per_device(): pl.pallas_call(functools.partial(near_kernel, rows=rows, n_samp=n_samp),...  1.21 us
    ppermute x1, waiting for transfers between devices, per_device(): lax.ppermute(fars[d], 'samp', [(i, (i + d) % n_samp) for i in range(n_sam...  1.09 us
    pallas_call x1, Pallas kernels, per_device(): pl.pallas_call(receive_kernel, out_shape=jax.ShapeDtypeStruct((leaf_count...  1 us
  transfers between devices with their start and end apart: 3, of which 1 were waited for; matrix products, arithmetic and copies ran while one was open for 2% of the time, Pallas kernels for 22%

profile of v2, /device:TPU:0, one launch (start us, length us, event | category | flops | bytes accessed | tf_op | source)
XLA Modules:
  0.0 26.5 jit_solution(421404051743038301)
XLA Ops:
  0.0 0.0 copy-start.1
  0.0 0.0 copy-start.3
  0.0 2.2 %radiate.1 = (bf16[4,80,128]{2,1,0:T(8,128)(2,1)S(1)}, bf16[8,2,4096]{2,1,0:T(2,128)(2,1)S(1)}, bf16[32,2,4096]{2,1,0:T(2,128)(2,1)S(1)}) custom-call(s32[8]{0:T(128)} %parent_hbm.3, s32[8]{0:T(128)} %sid_hbm.1, bf16[4,8,128]{2,1,0:T(8,128)(2,1)} %cur_hbm.1, bf16[4,2,2,512,128]{4,3,2,1,0:T(8,128)(2,1)} %rad_ref.1, bf16[8,2,4096]{2,1,0:T(2,128)(2,1)} %phase_hbm.1, ...), custom_call_target="tpu_custom_call" | custom-call | tf_op jit(solution)/shard_map/radiate/pallas_call | solution.py:449
  2.2 2.0 %all-gather = bf16[8,80,128]{2,1,0:T(8,128)(2,1)S(1)} all-gather(bf16[4,80,128]{2,1,0:T(8,128)(2,1)S(1)} %get-tuple-element.19), channel_id=2, replica_groups=mesh['box'=16,'samp'=2] {'samp'}, dimensions={0}, use_global_device_ids=true | all-gather | bytes 245760 | tf_op jit(solution)/shard_map/all_gather | solution.py:473
  4.2 0.7 %collective-permute-start = (bf16[2,4,80,128]{3,2,1,0:T(8,128)(2,1)S(1)}, bf16[2,4,80,128]{3,2,1,0:T(8,128)(2,1)S(1)}, u32[]{:S(2)}, u32[]{:S(2)}) collective-permute-start(bf16[2,4,80,128]{3,2,1,0:T(8,128)(2,1)S(1)} %bitcast.2), channel_id=1, source_target_pairs={{1,2},{2,1},{3,4},{4,3},{5,6},{6,5},{7,8},{8,7},{9,10},{10,9},{11,... | collective-permute-start | bytes 491528 | tf_op jit(solution)/shard_map/ppermute | solution.py:479
  4.9 0.1 reshape.15.shift_ref
  5.0 0.3 %reshape.17.trans_ref = f32[64,32,128]{2,1,0:T(8,128)S(1)} reshape(bf16[32,2,4096]{2,1,0:T(2,128)(2,1)S(1)} %get-tuple-element.21) | data formatting | bytes 1572864 | tf_op jit(solution)/shard_map/reshape | solution.py:481
  5.3 0.0 copy-done.1
  5.3 0.0 copy-done.3
  5.3 0.0 copy-start.2
  5.4 4.7 %tables.1 = (bf16[4096,512]{1,0:T(8,128)(2,1)S(1)}, f32[16,32,8,128]{3,2,1,0:T(8,128)S(1)}, f32[66,32,8,128]{3,2,1,0:T(8,128)S(1)}, f32[24,2,32,8,128]{4,3,2,1,0:T(8,128)S(1)}, bf16[4,8,2,128,128]{4,3,2,1,0:T(8,128)(2,1)S(1)}) custom-call(s32[2,32]{1,0:T(2,128)S(1)} %bitcast.6, s32[8]{0:T(128)S(1)} %copy-done.1, bf16[32,2,128,128]{3,2,1,0:T(8,128)(2,1)} %val_hbm.1, ...), custom_call_target="tpu_custom_call" | custom-call | flops 1610612736 | bytes 16777216 | tf_op jit(solution)/shard_map/tables/pallas_call | solution.py:484
  10.0 0.0 collective-permute-done.rest_0_.near_ref
  10.0 4.3 %collective-permute-start.1 = (bf16[2,4,80,128]{3,2,1,0:T(8,128)(2,1)S(1)}, bf16[2,4,80,128]{3,2,1,0:T(8,128)(2,1)S(1)}, u32[]{:S(2)}, u32[]{:S(2)}) collective-permute-start(bf16[2,4,80,128]{3,2,1,0:T(8,128)(2,1)S(1)} %collective-permute-done.rest_0_.near_ref), channel_id=1, source_target_pairs={{0,1},{1,0},{2,3},{3,2},{4,5},{5,4},{6,7},{7,6},{8,9},{9,8},{10,11... | collective-permute-start | bytes 491528 | tf_op jit(solution)/shard_map/ppermute | solution.py:503
  14.3 0.0 copy-done.2
  14.3 1.2 %near.1.near_ref = f32[4,8,128]{2,1,0:T(8,128)S(1)} custom-call(s32[4,8]{1,0:T(4,128)S(1)} %copy-done.2, bf16[4,8,2,128,128]{4,3,2,1,0:T(8,128)(2,1)S(1)} %get-tuple-element.24.near_ref, bf16[2,4,80,128]{3,2,1,0:T(8,128)(2,1)S(1)} %bitcast.4, bf16[2,4,80,128]{3,2,1,0:T(8,128)(2,1)S(1)} %collective-permute-done.rest_0_.near_ref), custom_call_target="tpu_custom_call" | custom-call | flops 1610612736 | bytes 4194304 | tf_op jit(solution)/shard_map/near/pallas_call | solution.py:509
  15.5 0.0 collective-permute-done.1.far_ref
  15.5 0.0 copy-start
  15.5 8.6 %field.1 = (bf16[4,64,128]{2,1,0:T(8,128)(2,1)S(1)}, bf16[4,64,128]{2,1,0:T(8,128)(2,1)S(1)}, f32[24,2,32,8,128]{4,3,2,1,0:T(8,128)S(1)}) custom-call(s32[8]{0:T(128)} %parent_hbm.3, s32[8]{0:T(128)} %sid_hbm.1, s32[16,16]{1,0:T(8,128)} %src_hbm.1, s32[16,16]{1,0:T(8,128)} %disp_hbm.1, ...), custom_call_target="tpu_custom_call", output_to_operand_aliasing={{2}: (10, {})} | custom-call | tf_op jit(solution)/shard_map/field/pallas_call | solution.py:521
  24.1 0.2 collective-permute-start.2
  24.4 1.1 %collective-permute-done.2.rest_1_ = bf16[4,64,128]{2,1,0:T(8,128)(2,1)S(1)} collective-permute-done((bf16[4,64,128]{2,1,0:T(8,128)(2,1)S(1)}, bf16[4,64,128]{2,1,0:T(8,128)(2,1)S(1)}, u32[]{:S(2)}, u32[]{:S(2)}) %collective-permute-start.2) | collective-permute-done | bytes 65568 | tf_op jit(solution)/shard_map/ppermute | solution.py:557
  25.5 0.0 copy-done
  25.5 1.0 %receive.1 = f32[4,8,128]{2,1,0:T(8,128)} custom-call(f32[4,8,128]{2,1,0:T(8,128)S(1)} %near.1.near_ref, bf16[4,2,2,512,128]{4,3,2,1,0:T(8,128)(2,1)S(1)} %copy-done, bf16[4,64,128]{2,1,0:T(8,128)(2,1)S(1)} %get-tuple-element.31.rest_0_, bf16[4,64,128]{2,1,0:T(8,128)(2,1)S(1)} %collective-permute-done.2.rest_1_), custom_call_target="tpu_custom_call" | custom-call | tf_op jit(solution)/shard_map/receive/pallas_call | solution.py:560
Async XLA Ops:
  0.0 5.3 %copy-start.1 = (s32[8]{0:T(128)S(1)}, s32[8]{0:T(128)}, u32[]{:S(2)}) copy-start(s32[8]{0:T(128)} %sid_hbm.1) | copy-start | bytes 100
  0.0 5.3 %copy-start.3 = (s32[32,2]{0,1:T(2,128)S(1)}, s32[32,2]{0,1:T(2,128)}, u32[]{:S(2)}) copy-start(s32[32,2]{0,1:T(2,128)} %param.19) | copy-start | bytes 772
  4.2 5.8 %collective-permute-start = (bf16[2,4,80,128]{3,2,1,0:T(8,128)(2,1)S(1)}, bf16[2,4,80,128]{3,2,1,0:T(8,128)(2,1)S(1)}, u32[]{:S(2)}, u32[]{:S(2)}) collective-permute-start(bf16[2,4,80,128]{3,2,1,0:T(8,128)(2,1)S(1)} %bitcast.2), channel_id=1, source_target_pairs={{1,2},{2,1},{3,4},{4,3},{5,6},{6,5},{7,8},{8,7},{9,10},{10,9},{11,... | collective-permute-start | bytes 491528 | tf_op jit(solution)/shard_map/ppermute | solution.py:479
  5.3 8.9 %copy-start.2 = (s32[4,8]{1,0:T(4,128)S(1)}, s32[4,8]{1,0:T(4,128)}, u32[]{:S(2)}) copy-start(s32[4,8]{1,0:T(4,128)} %src_ref.1) | copy-start | bytes 388
  10.0 5.5 %collective-permute-start.1 = (bf16[2,4,80,128]{3,2,1,0:T(8,128)(2,1)S(1)}, bf16[2,4,80,128]{3,2,1,0:T(8,128)(2,1)S(1)}, u32[]{:S(2)}, u32[]{:S(2)}) collective-permute-start(bf16[2,4,80,128]{3,2,1,0:T(8,128)(2,1)S(1)} %collective-permute-done.rest_0_.near_ref), channel_id=1, source_target_pairs={{0,1},{1,0},{2,3},{3,2},{4,5},{5,4},{6,7},{7,6},{8,9},{9,8},{10,11... | collective-permute-start | bytes 491528 | tf_op jit(solution)/shard_map/ppermute | solution.py:503
  15.5 10.0 %copy-start = (bf16[4,2,2,512,128]{4,3,2,1,0:T(8,128)(2,1)S(1)}, bf16[4,2,2,512,128]{4,3,2,1,0:T(8,128)(2,1)}, u32[]{:S(2)}) copy-start(bf16[4,2,2,512,128]{4,3,2,1,0:T(8,128)(2,1)} %rad_ref.1) | copy-start | bytes 6291460
  24.1 1.3 %collective-permute-start.2 = (bf16[4,64,128]{2,1,0:T(8,128)(2,1)S(1)}, bf16[4,64,128]{2,1,0:T(8,128)(2,1)S(1)}, u32[]{:S(2)}, u32[]{:S(2)}) collective-permute-start(bf16[4,64,128]{2,1,0:T(8,128)(2,1)S(1)} %get-tuple-element.32), channel_id=1, source_target_pairs={{0,1},{1,0},{2,3},{3,2},{4,5},{5,4},{6,7},{7,6},{8,9},{9,8},{10,11... | collective-permute-start | bytes 196616 | tf_op jit(solution)/shard_map/ppermute | solution.py:557
